TPU v7x, 256 devices: a whole 4x4x8 slice. The times are simulated.
256 devices in a mesh: expert: 32 (over y, x, core), tensor: 8 (over z).
Axes of the slice: x: 4, y: 4, z: 8, core: 2. Of those that a mesh axis runs over, the one named last changes fastest.
Arguments:
- tokens: bfloat16 [16384, 4096], P('expert', 'tensor'), may hold values from -36 to 36
- expert_ids: int32 [16384, 1], P('expert'), may hold values from 0 to 63; in each aligned block of 512 rows (0 to 511, 512 to 1023, ...) at most 16 rows name the same one
- gates: float32 [16384, 1], P('expert'), may hold values from 0.25 to 1
- expert_in: bfloat16 [64, 4096, 2048], P('expert', 'tensor'), may hold values from -0.09375 to 0.09375
- expert_out: bfloat16 [64, 2048, 4096], P('expert', None, 'tensor'), may hold values from -0.125 to 0.125
- norm_gain: float32 [4096], replicated, may hold values from 0.5 to 2
- up_weight: bfloat16 [4096, 8192], P('expert', 'tensor'), may hold values from -0.09375 to 0.09375
- down_weight: bfloat16 [4096, 8192], P('expert', 'tensor'), may hold values from -0.0625 to 0.0625
Outputs:
- layer_output: bfloat16 [16384, 4096], P('expert', 'tensor')
Inputs may be any that keep to these rules, and one draw needn't show every extreme that they name: `expert_ids`: among the 512 tokens of one block, at most 16 carry the same expert id; in some blocks one id is carried by exactly 16 tokens.
All inputs are finite; a program needn't handle non-finite values.
Results may differ from a plain program's by a relative error of at most 0.015.
Values may be sent and summed in bfloat16 or wider, within the bound.
No kernel may reach another device: no remote copies, remote signals or barrier semaphores. Data moves between devices by JAX's collectives and lax.ppermute only.
A program may use at most 128 MiB of HBM per device.

v0:
```python
import jax
import jax.numpy as jnp
from jax import lax
from jax.sharding import PartitionSpec as P

EXP_DEV = 2


def slot_table(expert_col, experts, capacity):
    expert = expert_col[:, 0]
    onehot = (expert[:, None] == jnp.arange(experts, dtype=jnp.int32)[None, :]).astype(jnp.int32)
    before = jnp.cumsum(onehot, axis=0) - onehot
    position = jnp.sum(before * onehot, axis=1)
    slot_index = expert * capacity + position
    selector = jnp.arange(experts * capacity, dtype=jnp.int32)[:, None] == slot_index[None, :]
    return selector.astype(jnp.bfloat16)


def trade(buffer):
    result = lax.all_to_all(buffer, "expert", split_axis=0, concat_axis=0, tiled=True)
    return result


def gather_rows(weight, combine, start_value):
    return combine(start_value, lax.all_gather(weight, "expert", axis=0, tiled=True), jnp.int32(0))


def shards(tokens, expert_ids, gates, expert_in, expert_out, norm_gain, up_weight, down_weight):
    token_count = tokens.shape[0]
    local_width = tokens.shape[1]
    groups = lax.axis_size("expert")
    experts = EXP_DEV * groups
    capacity = 2 * token_count // experts
    selector = slot_table(expert_ids, experts, capacity)
    outgoing = jnp.dot(selector, tokens, preferred_element_type=jnp.float32).astype(jnp.bfloat16)
    outgoing = outgoing.reshape(groups, EXP_DEV, capacity, local_width)
    arrived = trade(outgoing)
    partial_value = jnp.einsum(
        "sjcd,jdh->sjch", arrived, expert_in, preferred_element_type=jnp.float32
    )
    summed = lax.psum(partial_value.astype(jnp.bfloat16), "tensor").astype(jnp.float32)
    active = jax.nn.relu(summed).astype(jnp.bfloat16)
    produced = jnp.einsum(
        "sjch,jhd->sjcd", active, expert_out, preferred_element_type=jnp.float32
    ).astype(jnp.bfloat16)
    returned = trade(produced).reshape(experts * capacity, local_width)
    routed = lax.dot_general(
        selector, returned, (((0,), (0,)), ((), ())), preferred_element_type=jnp.float32
    )
    mixed = (tokens.astype(jnp.float32) + gates * routed).astype(jnp.bfloat16)
    whole = lax.all_gather(mixed, "tensor", axis=1, tiled=True)
    whole_f32 = whole.astype(jnp.float32)
    mean_square = jnp.mean(whole_f32 * whole_f32, axis=1, keepdims=True)
    normed = (whole_f32 * lax.rsqrt(mean_square + 1e-06) * norm_gain).astype(jnp.bfloat16)

    def add_up(carry, piece, start):
        return jnp.dot(normed, piece, preferred_element_type=jnp.float32)

    ffn_hidden = gather_rows(
        up_weight, add_up, jnp.zeros((token_count, up_weight.shape[1]), jnp.float32)
    )
    ffn_active = jax.nn.gelu(ffn_hidden, approximate=True).astype(jnp.bfloat16)

    def add_down(carry, piece, start):
        contribution = lax.dot_general(
            ffn_active, piece, (((1,), (1,)), ((), ())), preferred_element_type=jnp.float32
        )
        return contribution

    outputs = gather_rows(
        down_weight, add_down, jnp.zeros((token_count, whole.shape[1]), jnp.float32)
    )
    summed_out = lax.psum_scatter(
        outputs.astype(jnp.bfloat16), "tensor", scatter_dimension=1, tiled=True
    ).astype(jnp.float32)
    return (mixed.astype(jnp.float32) + summed_out).astype(jnp.bfloat16)


def solution(mesh):
    return jax.shard_map(
        shards,
        mesh=mesh,
        in_specs=(
            P("expert", "tensor"),
            P("expert", None),
            P("expert", None),
            P("expert", "tensor", None),
            P("expert", None, "tensor"),
            P(),
            P("expert", "tensor"),
            P("expert", "tensor"),
        ),
        out_specs=P("expert", "tensor"),
        check_vma=False,
    )
```

profile of v0, /device:TPU:1, one launch (start us, length us, event | category | flops | bytes accessed | tf_op | source)
XLA Modules:
  0.0 424.8 jit_solution(10991581283528540992)
XLA Ops:
  6.5 0.7 fusion.42
  7.2 1.2 reduce-window.6
  8.4 0.2 slice_reduce_fusion
  8.7 0.9 fusion.41
  9.7 0.9 multiply_add_fusion
  10.6 1.8 fusion.24
  12.4 25.6 %all_to_all.10 = bf16[32,2,16,512]{3,2,1,0:T(8,128)(2,1)S(1)} all-to-all(bf16[32,2,16,512]{3,2,1,0:T(8,128)(2,1)S(1)} %bitcast.50), channel_id=1, replica_groups=mesh['expert'=32,'tensor'=8] {'expert'}, dimensions={0} | all-to-all | bytes 2097152 | tf_op jit(solution)/shard_map/all_to_all | solution.py:20
  37.9 4.3 %convert_bitcast_fusion = bf16[32,2,16,2048]{3,2,0,1:T(8,128)(2,1)} fusion(bf16[2,512,2048]{2,1,0:T(8,128)(2,1)S(1)} %copy-done.1, bf16[32,2,16,512]{3,2,1,0:T(8,128)(2,1)S(1)} %all_to_all.10), kind=kOutput, calls=%fused_computation.15 | convolution fusion | flops 2149580800 | bytes 9437184 | tf_op jit(solution)/shard_map/sjcd,jdh->sjch/dot_general | solution.py:38
  42.2 0.0 all-reduce.2.cloned.1.call-update
  42.3 0.0 all-gather.4.cloned.1.call-start
  42.3 108.1 %all-reduce.2.cloned.1.call-done = bf16[32,2,16,2048]{3,2,0,1:T(8,128)(2,1)} async-done(((bf16[32,2,16,2048]{3,2,0,1:T(8,128)(2,1)}), bf16[32,2,16,2048]{3,2,0,1:T(8,128)(2,1)}) %all-reduce.2.cloned.1.call-update) | async-done | bytes 4194320 | tf_op jit(solution)/shard_map/psum | solution.py:41
  150.4 5.8 %fusion.30 = bf16[32,2,16,512]{3,2,0,1:T(8,128)(2,1)S(1)} fusion(bf16[2,2048,512]{2,1,0:T(8,128)(2,1)} %param.12, bf16[32,2,16,2048]{3,2,0,1:T(8,128)(2,1)} %all-reduce.2.cloned.1.call-done), kind=kOutput, calls=%fused_computation.30 | convolution fusion | flops 2154299392 | bytes 9437184 | tf_op jit(solution)/shard_map/sjch,jhd->sjcd/dot_general | solution.py:43
  156.2 0.0 copy-start.2
  156.2 0.0 copy-start.4
  156.2 0.1 copy.16
  156.3 24.6 %all_to_all.11 = bf16[32,2,16,512]{3,2,1,0:T(8,128)(2,1)S(1)} all-to-all(bf16[32,2,16,512]{3,2,1,0:T(8,128)(2,1)S(1)} %copy.16), channel_id=1, replica_groups=mesh['expert'=32,'tensor'=8] {'expert'}, dimensions={0} | all-to-all | bytes 2097152 | tf_op jit(solution)/shard_map/all_to_all | solution.py:20
  180.9 1.6 fusion.35
  182.5 0.0 all-gather.4.cloned.1.call-update
  182.5 0.0 all-gather.6.cloned.1.call-start
  182.6 0.7 all-gather.6.cloned.1.call-update
  183.3 0.0 all-gather.8.cloned.1.call-start
  183.3 0.5 all-gather.8.cloned.1.call-update
  183.8 0.2 reduce-scatter.2.cloned.1.call-start
  184.1 48.4 %all-gather.4.cloned.1.call-done = bf16[512,4096]{1,0:T(8,128)(2,1)} async-done(((bf16[512,512]{1,0:T(8,128)(2,1)}), bf16[512,4096]{1,0:T(8,128)(2,1)}) %all-gather.4.cloned.1.call-update) | async-done | bytes 4194320 | tf_op jit(solution)/shard_map/all_gather | solution.py:51
  232.4 3.1 fusion
  235.5 56.4 %all-gather.6.cloned.1.call-done = bf16[4096,1024]{1,0:T(8,128)(2,1)} async-done(((bf16[128,1024]{1,0:T(8,128)(2,1)}), bf16[4096,1024]{1,0:T(8,128)(2,1)}) %all-gather.6.cloned.1.call-update) | async-done | bytes 8388624 | tf_op jit(solution)/shard_map/all_gather | solution.py:25
  292.0 9.6 %fusion.21 = bf16[512,1024]{1,0:T(8,128)(2,1)S(1)} fusion(bf16[4096,1024]{1,0:T(8,128)(2,1)} %all-gather.6.cloned.1.call-done, bf16[512,4096]{1,0:T(8,128)(2,1)} %all-gather.4.cloned.1.call-done, f32[4096]{0:T(1024)S(1)} %copy-done.3, f32[512]{0:T(512)S(1)} %add_rsqrt_fusion), kind=kOutput, calls=%fused_computation.24 | convolution fusion | flops 4308074496 | bytes 13649920 | tf_op jit(solution)/shard_map/dot_general | solution.py:57
  301.6 50.4 %all-gather.8.cloned.1.call-done = bf16[4096,1024]{1,0:T(8,128)(2,1)} async-done(((bf16[128,1024]{1,0:T(8,128)(2,1)}), bf16[4096,1024]{1,0:T(8,128)(2,1)}) %all-gather.8.cloned.1.call-update) | async-done | bytes 8388624 | tf_op jit(solution)/shard_map/all_gather | solution.py:25
  352.0 9.5 %convolution_convert_fusion = bf16[512,4096]{1,0:T(8,128)(2,1)} fusion(bf16[512,1024]{1,0:T(8,128)(2,1)S(1)} %fusion.21, bf16[4096,1024]{1,0:T(8,128)(2,1)} %all-gather.8.cloned.1.call-done), kind=kOutput, calls=%fused_computation.6 | convolution fusion | flops 4297064448 | bytes 13631488 | tf_op jit(solution)/shard_map/dot_general | solution.py:65
  361.5 0.0 reduce-scatter.2.cloned.1.call-update
  361.5 54.7 %reduce-scatter.2.cloned.1.call-done = bf16[512,512]{1,0:T(8,128)(2,1)} async-done(((bf16[512,4096]{1,0:T(8,128)(2,1)}), bf16[512,512]{1,0:T(8,128)(2,1)}) %reduce-scatter.2.cloned.1.call-update) | async-done | bytes 524304 | tf_op jit(solution)/shard_map/reduce_scatter | solution.py:73
  416.3 2.0 add_convert_fusion
  (12 shorter events, 0.1 us)
Async XLA Ops:
  6.5 143.8 %all-reduce.2.cloned.1.call-start = ((), (), s32[]{:S(2)}) async-start(), calls=%async_computation.3 | async-start | bytes 8388608 | tf_op jit(solution)/shard_map/psum | solution.py:41
  8.7 29.2 %copy-start.1 = (bf16[2,512,2048]{2,1,0:T(8,128)(2,1)S(1)}, bf16[2,512,2048]{2,1,0:T(8,128)(2,1)}, u32[]{:S(2)}) copy-start(bf16[2,512,2048]{2,1,0:T(8,128)(2,1)} %param.11) | copy-start | bytes 12582916
  42.3 190.2 %all-gather.4.cloned.1.call-start = ((), (), s32[]{:S(2)}) async-start(), calls=%async_computation.4 | async-start | bytes 4718592 | tf_op jit(solution)/shard_map/all_gather | solution.py:51
  156.2 24.7 %copy-start.2 = (bf16[512,512]{1,0:T(8,128)(2,1)S(1)}, bf16[512,512]{1,0:T(8,128)(2,1)}, u32[]{:S(2)}) copy-start(bf16[512,512]{1,0:T(8,128)(2,1)} %param.8) | copy-start | bytes 1572868
  156.2 24.7 %copy-start.4 = (f32[512,1]{0,1:T(1,128)S(1)}, f32[512,1]{0,1:T(1,128)}, u32[]{:S(2)}) copy-start(f32[512,1]{0,1:T(1,128)} %param.10) | copy-start | bytes 6148
  180.9 111.0 %copy-start.3 = (f32[4096]{0:T(1024)S(1)}, f32[4096]{0:T(1024)}, u32[]{:S(2)}) copy-start(f32[4096]{0:T(1024)} %param.13) | copy-start | bytes 49156
  182.5 109.4 %all-gather.6.cloned.1.call-start = ((), (), s32[]{:S(2)}) async-start(), calls=%async_computation.5 | async-start | bytes 8650752 | tf_op jit(solution)/shard_map/all_gather | solution.py:25
  183.3 168.7 %all-gather.8.cloned.1.call-start = ((), (), s32[]{:S(2)}) async-start(), calls=%async_computation.6 | async-start | bytes 8650752 | tf_op jit(solution)/shard_map/all_gather | solution.py:25
  183.8 232.4 %reduce-scatter.2.cloned.1.call-start = ((), (), s32[]{:S(2)}) async-start(), calls=%async_computation.7 | async-start | bytes 4718592 | tf_op jit(solution)/shard_map/reduce_scatter | solution.py:73
  361.5 54.8 %copy-start = (bf16[512,512]{1,0:T(8,128)(2,1)S(1)}, bf16[512,512]{1,0:T(8,128)(2,1)}, u32[]{:S(2)}) copy-start(bf16[512,512]{1,0:T(8,128)(2,1)} %fusion.35) | copy-start | bytes 1572868
Sparse Core Ops, SparseCore 0:
  42.4 107.9 all-reduce.1
  182.6 49.7 all-gather.3
  235.0 56.9 all-gather.5
  294.4 57.5 all-gather.7
  361.6 54.5 reduce-scatter.1
where the time goes:
time: 425 us
  waiting for transfers between devices  319 us (75%)
  blocking collectives  50.2 us (12%)
  matrix products  32.6 us (8%)
  between operations  13.2 us (3%)
  other arithmetic  8.86 us (2%)
    psum x1, waiting for transfers between devices, shards(): lax.psum(partial_value.astype(jnp.bfloat16), 'tensor').astype(jnp.float32)  108 us
    all_gather x2, waiting for transfers between devices, gather_rows(): lax.all_gather(weight, 'expert', axis=0, tiled=True)  107 us
    reduce_scatter x1, waiting for transfers between devices, shards(): lax.psum_scatter(outputs.astype(jnp.bfloat16), 'tensor', scatter_dimensio...  54.7 us
    all_to_all x2, blocking collectives, trade(): lax.all_to_all(buffer, 'expert', split_axis=0, concat_axis=0, tiled=True)  50.2 us
    all_gather x1, waiting for transfers between devices, shards(): whole = lax.all_gather(mixed, 'tensor', axis=1, tiled=True)  48.4 us
    dot_general x1, matrix products, add_up(): return jnp.dot(normed, piece, preferred_element_type=jnp.float32)  9.58 us
    dot_general x1, matrix products, add_down(): lax.dot_general(ffn_active, piece, (((1,), (1,)), ((), ())), preferred_el...  9.54 us
  transfers between devices with their start and end apart: 5, of which 5 were waited for; matrix products, arithmetic and copies ran while one was open for 3% of the time, Pallas kernels for 0%

commit v1 on v0

--- a/solution.py
+++ b/solution.py
@@ -48,7 +48,23 @@
         selector, returned, (((0,), (0,)), ((), ())), preferred_element_type=jnp.float32
     )
     mixed = (tokens.astype(jnp.float32) + gates * routed).astype(jnp.bfloat16)
-    whole = lax.all_gather(mixed, "tensor", axis=1, tiled=True)
+    ways, here, turn = (lax.axis_size("tensor"), lax.axis_index("tensor"), mixed.shape[1])
+    shape = [n * ways if d == 1 else n for d, n in enumerate(mixed.shape)]
+    full = lax.dynamic_update_slice_in_dim(
+        jnp.zeros(shape, mixed.dtype), mixed, here * turn, axis=1
+    )
+    going_up = going_down = mixed
+    for far in range(1, ways // 2 + 1):
+        going_up = lax.ppermute(going_up, "tensor", [(d, (d + 1) % ways) for d in range(ways)])
+        full = lax.dynamic_update_slice_in_dim(full, going_up, (here - far) % ways * turn, axis=1)
+        if 2 * far < ways:
+            going_down = lax.ppermute(
+                going_down, "tensor", [(d, (d - 1) % ways) for d in range(ways)]
+            )
+            full = lax.dynamic_update_slice_in_dim(
+                full, going_down, (here + far) % ways * turn, axis=1
+            )
+    whole = full
     whole_f32 = whole.astype(jnp.float32)
     mean_square = jnp.mean(whole_f32 * whole_f32, axis=1, keepdims=True)
     normed = (whole_f32 * lax.rsqrt(mean_square + 1e-06) * norm_gain).astype(jnp.bfloat16)

time: 425 us -> 329 us (0.77)
  waiting for transfers between devices: 319 us -> 220 us
  blocking collectives: 50.2 us -> 25.6 us
  starting transfers between devices: 0.34 us -> 15.8 us
  local copies, waits for them, and re-layouts: 0.33 us -> 10.5 us
    all_gather x2, waiting for transfers between devices: 107 us -> 0.05 us  [gather_rows(): lax.all_gather(weight, 'expert', axis=0, tiled=True)]
    all_gather x1 -> x0, waiting for transfers between devices: 48.4 us -> none  [shards(): whole = lax.all_gather(mixed, 'tensor', axis=1, tiled=True)]
    ppermute x0 -> x7, waiting for transfers between devices: none -> 38.7 us  [the longest x4 38.7 us: shards(): lax.ppermute(going_up, 'tensor', [(d, (d + 1) % ways) for d in range(ways)])]
    all_to_all x2 -> x1, blocking collectives: 50.2 us -> 25.6 us  [trade(): lax.all_to_all(buffer, 'expert', split_axis=0, concat_axis=0, tiled=True)]
    all_to_all x0 -> x1, waiting for transfers between devices: none -> 16.9 us  [trade(): lax.all_to_all(buffer, 'expert', split_axis=0, concat_axis=0, tiled=True)]
    ppermute x0 -> x7, starting transfers between devices: none -> 8.03 us  [the longest x3 8.02 us: shards(): lax.ppermute(going_down, 'tensor', [(d, (d - 1) % ways) for d in range(wa...]
    all_to_all x0 -> x1, starting transfers between devices: none -> 7.69 us  [trade(): lax.all_to_all(buffer, 'expert', split_axis=0, concat_axis=0, tiled=True)]
    dynamic_update_slice x0 -> x7, local copies, waits for them, and re-layouts: none -> 5.8 us  [the longest x4 3.32 us: shards(): lax.dynamic_update_slice_in_dim(full, going_up, (here - far) % ways * tur...]
  transfers between devices with their start and end apart: 5 -> 12, of which waited for: 5 -> 7; matrix products, arithmetic and copies ran while one was open for 3% -> 9% of each run, Pallas kernels for 0% -> 0%
where the time goes in v1:
time: 329 us; the launch traced here: 328 us
  waiting for transfers between devices  220 us (67%)
  matrix products  33 us (10%)
  blocking collectives  25.6 us (8%)
  starting transfers between devices  15.8 us (5%)
  between operations  15 us (5%)
  local copies, waits for them, and re-layouts  10.5 us (3%)
  other arithmetic  8.12 us (2%)
    psum x1, waiting for transfers between devices, shards(): lax.psum(partial_value.astype(jnp.bfloat16), 'tensor').astype(jnp.float32)  107 us
    reduce_scatter x1, waiting for transfers between devices, shards(): lax.psum_scatter(outputs.astype(jnp.bfloat16), 'tensor', scatter_dimensio...  56.7 us
    ppermute x4, waiting for transfers between devices, shards(): lax.ppermute(going_up, 'tensor', [(d, (d + 1) % ways) for d in range(ways)])  38.7 us
    all_to_all x1, blocking collectives, trade(): lax.all_to_all(buffer, 'expert', split_axis=0, concat_axis=0, tiled=True)  25.6 us
    all_to_all x1, waiting for transfers between devices, trade(): lax.all_to_all(buffer, 'expert', split_axis=0, concat_axis=0, tiled=True)  16.9 us
    dot_general x1, matrix products, add_up(): return jnp.dot(normed, piece, preferred_element_type=jnp.float32)  9.64 us
    dot_general x1, matrix products, add_down(): lax.dot_general(ffn_active, piece, (((1,), (1,)), ((), ())), preferred_el...  9.53 us
    ppermute x3, starting transfers between devices, shards(): lax.ppermute(going_down, 'tensor', [(d, (d - 1) % ways) for d in range(wa...  8.02 us
  transfers between devices with their start and end apart: 12, of which 7 were waited for; matrix products, arithmetic and copies ran while one was open for 9% of the time, Pallas kernels for 0%

profile of v1, /device:TPU:1, one launch (start us, length us, event | category | flops | bytes accessed | tf_op | source)
XLA Modules:
  0.0 328.4 jit_solution(6607001043702664230)
XLA Ops:
  8.1 1.2 reduce-window.6
  9.5 0.9 fusion.47
  10.5 0.9 multiply_add_fusion
  11.4 1.8 fusion.24
  13.2 25.6 %all_to_all.10 = bf16[32,2,16,512]{3,2,1,0:T(8,128)(2,1)S(1)} all-to-all(bf16[32,2,16,512]{3,2,1,0:T(8,128)(2,1)S(1)} %bitcast.54), channel_id=1, replica_groups=mesh['expert'=32,'tensor'=8] {'expert'}, dimensions={0} | all-to-all | bytes 2097152 | tf_op jit(solution)/shard_map/all_to_all | solution.py:20
  38.8 4.3 %convert_bitcast_fusion = bf16[32,2,16,2048]{3,2,0,1:T(8,128)(2,1)} fusion(bf16[2,512,2048]{2,1,0:T(8,128)(2,1)S(1)} %copy-done.1, bf16[32,2,16,512]{3,2,1,0:T(8,128)(2,1)S(1)} %all_to_all.10), kind=kOutput, calls=%fused_computation.15 | convolution fusion | flops 2149580800 | bytes 9437184 | tf_op jit(solution)/shard_map/sjcd,jdh->sjch/dot_general | solution.py:38
  44.3 106.9 %all-reduce.2.cloned.1.call-done = bf16[32,2,16,2048]{3,2,0,1:T(8,128)(2,1)} async-done(((bf16[32,2,16,2048]{3,2,0,1:T(8,128)(2,1)}), bf16[32,2,16,2048]{3,2,0,1:T(8,128)(2,1)}) %all-reduce.2.cloned.1.call-update) | async-done | bytes 4194320 | tf_op jit(solution)/shard_map/psum | solution.py:41
  151.2 6.1 %fusion.30 = bf16[32,2,16,512]{3,2,0,1:T(8,128)(2,1)S(1)} fusion(bf16[2,2048,512]{2,1,0:T(8,128)(2,1)} %param.12, bf16[32,2,16,2048]{3,2,0,1:T(8,128)(2,1)} %all-reduce.2.cloned.1.call-done), kind=kOutput, calls=%fused_computation.30 | convolution fusion | flops 2154299392 | bytes 9437184 | tf_op jit(solution)/shard_map/sjch,jhd->sjcd/dot_general | solution.py:43
  157.4 1.0 copy.26
  158.4 7.7 %all-to-all-start.1 = ((bf16[32,2,16,512]{3,2,1,0:T(8,128)(2,1)}), bf16[32,2,16,512]{3,2,1,0:T(8,128)(2,1)S(1)}, u32[]{:S(2)}, u32[]{:S(2)}) async-start(bf16[32,2,16,512]{3,2,1,0:T(8,128)(2,1)} %copy.26), calls=%async_computation.1 | async-start | bytes 2097152 | tf_op jit(solution)/shard_map/all_to_all | solution.py:20
  166.4 16.9 %all-to-all-done.1 = bf16[32,2,16,512]{3,2,1,0:T(8,128)(2,1)S(1)} async-done(((bf16[32,2,16,512]{3,2,1,0:T(8,128)(2,1)}), bf16[32,2,16,512]{3,2,1,0:T(8,128)(2,1)S(1)}, u32[]{:S(2)}, u32[]{:S(2)}) %all-to-all-start.1) | async-done | bytes 1048608 | tf_op jit(solution)/shard_map/all_to_all | solution.py:20
  183.3 2.2 broadcast_in_dim.2
  185.5 1.6 constant_dynamic-update-slice_fusion.7
  187.1 2.7 collective-permute-start.1
  189.8 11.6 %collective-permute-done = bf16[512,512]{0,1:T(8,128)(2,1)S(1)} collective-permute-done((bf16[512,512]{0,1:T(8,128)(2,1)S(1)}, bf16[512,512]{0,1:T(8,128)(2,1)S(1)}, u32[]{:S(2)}, u32[]{:S(2)}) %collective-permute-start) | collective-permute-done | bytes 524320 | tf_op jit(solution)/shard_map/ppermute | solution.py:58
  201.4 2.7 collective-permute-start.3
  204.1 10.7 %collective-permute-done.2 = bf16[512,512]{0,1:T(8,128)(2,1)S(1)} collective-permute-done((bf16[512,512]{0,1:T(8,128)(2,1)S(1)}, bf16[512,512]{0,1:T(8,128)(2,1)S(1)}, u32[]{:S(2)}, u32[]{:S(2)}) %collective-permute-start.2) | collective-permute-done | bytes 524320 | tf_op jit(solution)/shard_map/ppermute | solution.py:58
  214.8 2.7 collective-permute-start.5
  217.5 0.8 constant_dynamic-update-slice_fusion.6
  218.3 9.0 %collective-permute-done.4 = bf16[512,512]{0,1:T(8,128)(2,1)S(1)} collective-permute-done((bf16[512,512]{0,1:T(8,128)(2,1)S(1)}, bf16[512,512]{0,1:T(8,128)(2,1)S(1)}, u32[]{:S(2)}, u32[]{:S(2)}) %collective-permute-start.4) | collective-permute-done | bytes 524320 | tf_op jit(solution)/shard_map/ppermute | solution.py:58
  227.3 0.8 constant_dynamic-update-slice_fusion.5
  228.1 0.8 constant_dynamic-update-slice_fusion.4
  228.9 0.8 constant_dynamic-update-slice_fusion.3
  229.8 0.8 constant_dynamic-update-slice_fusion.2
  231.4 7.4 %collective-permute-done.6 = bf16[512,512]{0,1:T(8,128)(2,1)S(1)} collective-permute-done((bf16[512,512]{0,1:T(8,128)(2,1)S(1)}, bf16[512,512]{0,1:T(8,128)(2,1)S(1)}, u32[]{:S(2)}, u32[]{:S(2)}) %collective-permute-start.6) | collective-permute-done | bytes 524320 | tf_op jit(solution)/shard_map/ppermute | solution.py:58
  238.8 0.8 constant_dynamic-update-slice_fusion
  239.7 3.1 fusion
  242.8 9.6 %fusion.21.clone.4 = bf16[512,1024]{1,0:T(8,128)(2,1)S(1)} fusion(bf16[4096,1024]{1,0:T(8,128)(2,1)} %all-gather.3.cloned.1.call-done, bf16[512,4096]{0,1:T(8,128)(2,1)} %constant_dynamic-update-slice_fusion, f32[4096]{0:T(1024)S(1)} %copy-done.2, f32[512]{0:T(512)S(1)} %add_rsqrt_fusion), kind=kOutput, calls=%fused_computation.24.clone.clone.clone.1 | convolution fusion | flops 4308074496 | bytes 13649920 | tf_op jit(solution)/shard_map/dot_general | solution.py:73
  252.5 9.5 %convolution_convert_fusion = bf16[512,4096]{0,1:T(8,128)(2,1)} fusion(bf16[4096,1024]{1,0:T(8,128)(2,1)} %all-gather.5.cloned.1.call-done, bf16[512,1024]{1,0:T(8,128)(2,1)S(1)} %fusion.21.clone.4), kind=kOutput, calls=%fused_computation.6 | convolution fusion | flops 4297064448 | bytes 13631488 | tf_op jit(solution)/shard_map/dot_general | solution.py:81
  262.1 56.7 %reduce-scatter.2.cloned.1.call-done = bf16[512,512]{0,1:T(8,128)(2,1)} async-done(((bf16[512,4096]{0,1:T(8,128)(2,1)}), bf16[512,512]{0,1:T(8,128)(2,1)}) %reduce-scatter.2.cloned.1.call-update) | async-done | bytes 524304 | tf_op jit(solution)/shard_map/reduce_scatter | solution.py:89
  318.8 1.2 add_convert_fusion
  319.9 1.0 copy.28
  (32 shorter events, 3.3 us)
Async XLA Ops:
  7.4 143.8 %all-reduce.2.cloned.1.call-start = ((), (), s32[]{:S(2)}) async-start(), calls=%async_computation.3 | async-start | bytes 8388608 | tf_op jit(solution)/shard_map/psum | solution.py:41
  9.5 29.2 %copy-start.1 = (bf16[2,512,2048]{2,1,0:T(8,128)(2,1)S(1)}, bf16[2,512,2048]{2,1,0:T(8,128)(2,1)}, u32[]{:S(2)}) copy-start(bf16[2,512,2048]{2,1,0:T(8,128)(2,1)} %param.11) | copy-start | bytes 12582916
  43.1 199.7 %all-gather.3.cloned.1.call-start = ((), (), s32[]{:S(2)}) async-start(), calls=%async_computation.4 | async-start | bytes 8650752 | tf_op jit(solution)/shard_map/all_gather | solution.py:25
  43.7 208.8 %all-gather.5.cloned.1.call-start = ((), (), s32[]{:S(2)}) async-start(), calls=%async_computation.5 | async-start | bytes 8650752 | tf_op jit(solution)/shard_map/all_gather | solution.py:25
  157.3 8.8 %copy-start = (bf16[512,512]{1,0:T(8,128)(2,1)S(1)}, bf16[512,512]{1,0:T(8,128)(2,1)}, u32[]{:S(2)}) copy-start(bf16[512,512]{1,0:T(8,128)(2,1)} %param.8) | copy-start | bytes 1572868
  158.4 27.1 %copy-start.3 = (f32[512,1]{0,1:T(1,128)S(1)}, f32[512,1]{0,1:T(1,128)}, u32[]{:S(2)}) copy-start(f32[512,1]{0,1:T(1,128)} %param.10) | copy-start | bytes 6148
  158.4 24.9 %all-to-all-start.1 = ((bf16[32,2,16,512]{3,2,1,0:T(8,128)(2,1)}), bf16[32,2,16,512]{3,2,1,0:T(8,128)(2,1)S(1)}, u32[]{:S(2)}, u32[]{:S(2)}) async-start(bf16[32,2,16,512]{3,2,1,0:T(8,128)(2,1)} %copy.26), calls=%async_computation.1 | async-start | bytes 2097152 | tf_op jit(solution)/shard_map/all_to_all | solution.py:20
  166.1 152.7 %reduce-scatter.2.cloned.1.call-start = ((), (), s32[]{:S(2)}) async-start(), calls=%async_computation.6 | async-start | bytes 4718592 | tf_op jit(solution)/shard_map/reduce_scatter | solution.py:89
  187.1 14.3 %collective-permute-start = (bf16[512,512]{0,1:T(8,128)(2,1)S(1)}, bf16[512,512]{0,1:T(8,128)(2,1)S(1)}, u32[]{:S(2)}, u32[]{:S(2)}) collective-permute-start(bf16[512,512]{0,1:T(8,128)(2,1)S(1)} %get-tuple-element.6), channel_id=1, source_target_pairs={{0,1},{1,2},{2,3},{3,4},{4,5},{5,6},{6,7},{7,0},{8,9},{9,10},{10,1... | collective-permute-start | bytes 1572872 | tf_op jit(solution)/shard_map/ppermute | solution.py:58
  187.1 14.3 %collective-permute-start.1 = (bf16[512,512]{0,1:T(8,128)(2,1)S(1)}, bf16[512,512]{0,1:T(8,128)(2,1)S(1)}, u32[]{:S(2)}, u32[]{:S(2)}) collective-permute-start(bf16[512,512]{0,1:T(8,128)(2,1)S(1)} %get-tuple-element.6), channel_id=1, source_target_pairs={{0,7},{1,0},{2,1},{3,2},{4,3},{5,4},{6,5},{7,6},{8,15},{9,8},{10,9... | collective-permute-start | bytes 1572872 | tf_op jit(solution)/shard_map/ppermute | solution.py:61
  201.4 13.4 %collective-permute-start.2 = (bf16[512,512]{0,1:T(8,128)(2,1)S(1)}, bf16[512,512]{0,1:T(8,128)(2,1)S(1)}, u32[]{:S(2)}, u32[]{:S(2)}) collective-permute-start(bf16[512,512]{0,1:T(8,128)(2,1)S(1)} %collective-permute-done), channel_id=1, source_target_pairs={{0,1},{1,2},{2,3},{3,4},{4,5},{5,6},{6,7},{7,0},{8,9},{9,10},{10,1... | collective-permute-start | bytes 1572872 | tf_op jit(solution)/shard_map/ppermute | solution.py:58
  201.4 13.4 %collective-permute-start.3 = (bf16[512,512]{0,1:T(8,128)(2,1)S(1)}, bf16[512,512]{0,1:T(8,128)(2,1)S(1)}, u32[]{:S(2)}, u32[]{:S(2)}) collective-permute-start(bf16[512,512]{0,1:T(8,128)(2,1)S(1)} %collective-permute-done.1), channel_id=1, source_target_pairs={{0,7},{1,0},{2,1},{3,2},{4,3},{5,4},{6,5},{7,6},{8,15},{9,8},{10,9... | collective-permute-start | bytes 1572872 | tf_op jit(solution)/shard_map/ppermute | solution.py:61
  214.8 12.5 %collective-permute-start.4 = (bf16[512,512]{0,1:T(8,128)(2,1)S(1)}, bf16[512,512]{0,1:T(8,128)(2,1)S(1)}, u32[]{:S(2)}, u32[]{:S(2)}) collective-permute-start(bf16[512,512]{0,1:T(8,128)(2,1)S(1)} %collective-permute-done.2), channel_id=1, source_target_pairs={{0,1},{1,2},{2,3},{3,4},{4,5},{5,6},{6,7},{7,0},{8,9},{9,10},{10,1... | collective-permute-start | bytes 1572872 | tf_op jit(solution)/shard_map/ppermute | solution.py:58
  214.8 15.8 %collective-permute-start.5 = (bf16[512,512]{0,1:T(8,128)(2,1)S(1)}, bf16[512,512]{0,1:T(8,128)(2,1)S(1)}, u32[]{:S(2)}, u32[]{:S(2)}) collective-permute-start(bf16[512,512]{0,1:T(8,128)(2,1)S(1)} %collective-permute-done.3), channel_id=1, source_target_pairs={{0,7},{1,0},{2,1},{3,2},{4,3},{5,4},{6,5},{7,6},{8,15},{9,8},{10,9... | collective-permute-start | bytes 1572872 | tf_op jit(solution)/shard_map/ppermute | solution.py:61
  227.3 11.6 %collective-permute-start.6 = (bf16[512,512]{0,1:T(8,128)(2,1)S(1)}, bf16[512,512]{0,1:T(8,128)(2,1)S(1)}, u32[]{:S(2)}, u32[]{:S(2)}) collective-permute-start(bf16[512,512]{0,1:T(8,128)(2,1)S(1)} %collective-permute-done.4), channel_id=1, source_target_pairs={{0,1},{1,2},{2,3},{3,4},{4,5},{5,6},{6,7},{7,0},{8,9},{9,10},{10,1... | collective-permute-start | bytes 1572872 | tf_op jit(solution)/shard_map/ppermute | solution.py:58
  228.9 13.9 %copy-start.2 = (f32[4096]{0:T(1024)S(1)}, f32[4096]{0:T(1024)}, u32[]{:S(2)}) copy-start(f32[4096]{0:T(1024)} %param.13) | copy-start | bytes 49156
Sparse Core Ops, SparseCore 0:
  43.2 107.9 all-reduce.1
  262.2 56.5 reduce-scatter.1
Sparse Core Ops, SparseCore 1:
  46.1 57.1 all-gather.2
  105.7 57.4 all-gather.4
